TPU v7x, 128 devices: a whole 4x4x4 slice. The times are simulated.
128 devices in a mesh: fsdp: 32 (over y_hi, z, x), tensor: 4 (over y_lo, core).
Axes of the slice: x: 4, y: 4 (y_hi: 2, y_lo: 2; y = y_hi * 2 + y_lo), z: 4, core: 2. Of those that a mesh axis runs over, the one named last changes fastest.
Arguments:
- tokens: bfloat16 [2, 32, 256, 1024], P(None, 'fsdp', 'tensor'), may hold values from -6 to 6
- dealt: int32 [2, 32], P(None, 'fsdp'), may hold values 0 or 1
- cotangent: bfloat16 [2, 32, 256, 1024], P(None, 'fsdp', 'tensor'), may hold values from -6 to 6
- qkv_weight: bfloat16 [1, 1024, 3, 1024], P(None, 'fsdp', None, 'tensor'), may hold values from -0.1875 to 0.1875
- out_weight: bfloat16 [1, 1024, 1024], P(None, 'fsdp', 'tensor'), may hold values from -1.5 to 1.5
- up_weight: bfloat16 [1, 1024, 4096], P(None, 'fsdp', 'tensor'), may hold values from -0.1875 to 0.1875
- down_weight: bfloat16 [1, 1024, 4096], P(None, 'fsdp', 'tensor'), may hold values from -0.09375 to 0.09375
- norm1_gain: float32 [1, 1024], replicated, may hold values from 0.25 to 1.75
- norm1_bias: float32 [1, 1024], replicated, may hold values from -3 to 3
- query_bias: float32 [1, 1024], replicated, may hold values from -3 to 3
- value_bias: float32 [1, 1024], replicated, may hold values from -3 to 3
- out_bias: float32 [1, 1024], replicated, may hold values from -3 to 3
- norm2_gain: float32 [1, 1024], replicated, may hold values from 0.25 to 1.75
- norm2_bias: float32 [1, 1024], replicated, may hold values from -3 to 3
- up_bias: float32 [1, 4096], replicated, may hold values from -3 to 3
- down_bias: float32 [1, 1024], replicated, may hold values from -3 to 3
Outputs:
- block_out: bfloat16 [2, 32, 256, 1024], P(None, 'fsdp', 'tensor')
- input_grad: bfloat16 [2, 32, 256, 1024], P(None, 'fsdp', 'tensor')
- qkv_grad: float32 [1, 1024, 3, 1024], P(None, 'fsdp', None, 'tensor')
- out_grad: float32 [1, 1024, 1024], P(None, 'fsdp', 'tensor')
- up_grad: float32 [1, 1024, 4096], P(None, 'fsdp', 'tensor')
- down_grad: float32 [1, 1024, 4096], P(None, 'fsdp', 'tensor')
- norm1_gain_grad: float32 [1, 1024], replicated
- norm1_bias_grad: float32 [1, 1024], replicated
- query_bias_grad: float32 [1, 1024], replicated
- value_bias_grad: float32 [1, 1024], replicated
- out_bias_grad: float32 [1, 1024], replicated
- norm2_gain_grad: float32 [1, 1024], replicated
- norm2_bias_grad: float32 [1, 1024], replicated
- up_bias_grad: float32 [1, 4096], replicated
- down_bias_grad: float32 [1, 1024], replicated
Inputs may be any that keep to these rules, and one draw needn't show every extreme that they name: `dealt`: 1 where the slot holds an image of that micro-batch, 0 where it is empty.
All inputs are finite; a program needn't handle non-finite values. No bound on the sum of `dealt` on one device may be relied on, other than what follows from the above.
Results may differ from a plain program's by a relative error of at most 0.024.
Values may be sent and summed in bfloat16 or wider, within the bound.
No kernel may reach another device: no remote copies, remote signals or barrier semaphores. Data moves between devices by JAX's collectives and lax.ppermute only.
A program may use at most 64 MiB of HBM per device.

v0:
```python
import jax
import jax.numpy as jnp
from jax import lax
from jax.sharding import PartitionSpec as P

HEAD_DIM = 64
EPS_NORM = 1e-06


def layer_norm(values, gain, shift):
    center = values - jnp.mean(values, axis=-1, keepdims=True)
    spread = jnp.mean(center * center, axis=-1, keepdims=True)
    return center * lax.rsqrt(spread + EPS_NORM) * gain + shift


def split_heads(values):
    return values.reshape(values.shape[0], values.shape[1], -1, HEAD_DIM)


def row_total(values):
    return jnp.sum(values.astype(jnp.float32), axis=(0, 1))


def local(
    tokens,
    dealt,
    cotangent,
    qkv_weight,
    out_weight,
    up_weight,
    down_weight,
    norm1_gain,
    norm1_bias,
    query_bias,
    value_bias,
    out_bias,
    norm2_gain,
    norm2_bias,
    up_bias,
    down_bias,
):
    layer_count = qkv_weight.shape[0]
    micro_count = tokens.shape[0]
    slot_count = tokens.shape[1]
    local_rows = tokens.shape[2]
    model_width = tokens.shape[3]
    head_cols = qkv_weight.shape[3]
    unit_cols = up_weight.shape[2]
    unit_total = up_bias.shape[1]
    image_count = micro_count * slot_count
    tensor_index = lax.axis_index("tensor")
    score_scale = HEAD_DIM ** (-0.5)

    def spread_rows(block_rows):
        return lax.all_gather(block_rows, "tensor", axis=0, tiled=True)

    def spread_grads(block_rows):
        return lax.all_gather(block_rows, "tensor", axis=0, tiled=True)

    def collect_rows(term_fn):
        return lax.psum_scatter(
            term_fn(jnp.int32(0), local_rows * lax.axis_size("tensor")),
            "tensor",
            scatter_dimension=0,
            tiled=True,
        )

    def collect_grads(term_fn):
        return lax.psum_scatter(
            term_fn(jnp.int32(0), local_rows * lax.axis_size("tensor")),
            "tensor",
            scatter_dimension=0,
            tiled=True,
        )

    def vectors(layer):
        query_part = lax.dynamic_slice_in_dim(
            query_bias[layer], tensor_index * head_cols, head_cols, 0
        )
        value_part = lax.dynamic_slice_in_dim(
            value_bias[layer], tensor_index * head_cols, head_cols, 0
        )
        up_part = lax.dynamic_slice_in_dim(up_bias[layer], tensor_index * unit_cols, unit_cols, 0)
        return (
            norm1_gain[layer],
            norm1_bias[layer],
            query_part,
            value_part,
            out_bias[layer],
            norm2_gain[layer],
            norm2_bias[layer],
            up_part,
            down_bias[layer],
        )

    def inner_forward(hidden, weights, vecs):
        qkv_full, out_full, up_full, down_full = weights
        gain_one, shift_one, query_b, value_b, out_b, gain_two, shift_two, up_b, down_b = vecs
        normed = spread_rows(layer_norm(hidden, gain_one, shift_one).astype(jnp.bfloat16))
        joined = jnp.einsum("sid,dcf->sicf", normed, qkv_full, preferred_element_type=jnp.float32)
        query = (joined[:, :, 0] + query_b).astype(jnp.bfloat16)
        keys = joined[:, :, 1].astype(jnp.bfloat16)
        values = (joined[:, :, 2] + value_b).astype(jnp.bfloat16)
        scores = (
            jnp.einsum(
                "sihe,tihe->ihst",
                split_heads(query),
                split_heads(keys),
                preferred_element_type=jnp.float32,
            )
            * score_scale
        )
        probs = jax.nn.softmax(scores, axis=-1)
        mixed = jnp.einsum(
            "ihst,tihe->sihe",
            probs.astype(jnp.bfloat16),
            split_heads(values),
            preferred_element_type=jnp.float32,
        )
        mixed = mixed.reshape(query.shape).astype(jnp.bfloat16)

        def attn_term(start, count):
            return jnp.einsum("sid,ed->sie", mixed, out_full, preferred_element_type=jnp.float32)

        middle = hidden + (collect_rows(attn_term) + out_b)
        normed_two = spread_rows(layer_norm(middle, gain_two, shift_two).astype(jnp.bfloat16))
        upward = (
            jnp.einsum("sid,df->sif", normed_two, up_full, preferred_element_type=jnp.float32)
            + up_b
        )
        activated = jax.nn.gelu(upward, approximate=False).astype(jnp.bfloat16)
        return (normed, query, keys, values, probs, mixed, middle, normed_two, upward, activated)

    def backward_layer(hidden, grad_out, weights, vecs):
        qkv_full, out_full, up_full, down_full = weights
        gain_one, shift_one, query_b, value_b, out_b, gain_two, shift_two, up_b, down_b = vecs
        normed, query, keys, values, probs, mixed, middle, normed_two, upward, activated = (
            inner_forward(hidden, weights, vecs)
        )
        grad_down = grad_out.astype(jnp.bfloat16)
        down_b_grad = row_total(grad_down)
        down_all = spread_grads(grad_down)
        down_w_grad = jnp.einsum(
            "sie,sif->ef", down_all, activated, preferred_element_type=jnp.float32
        )
        grad_act = jnp.einsum(
            "sie,ef->sif", down_all, down_full, preferred_element_type=jnp.float32
        )
        gelu_value, gelu_pull = jax.vjp(lambda inner: jax.nn.gelu(inner, approximate=False), upward)
        grad_up = gelu_pull(grad_act)[0].astype(jnp.bfloat16)
        up_b_grad = row_total(grad_up)
        up_w_grad = jnp.einsum(
            "sid,sif->df", normed_two, grad_up, preferred_element_type=jnp.float32
        )

        def up_back(start, count):
            return jnp.einsum("sif,df->sid", grad_up, up_full, preferred_element_type=jnp.float32)

        norm_value, norm_pull = jax.vjp(layer_norm, middle, gain_two, shift_two)
        middle_part, gain_two_grad, shift_two_grad = norm_pull(collect_grads(up_back))
        grad_middle = grad_out + middle_part
        grad_att = grad_middle.astype(jnp.bfloat16)
        out_b_grad = row_total(grad_att)
        att_all = spread_grads(grad_att)
        out_w_grad = jnp.einsum("sie,sid->ed", att_all, mixed, preferred_element_type=jnp.float32)
        grad_mixed = jnp.einsum(
            "sie,ed->sid", att_all, out_full, preferred_element_type=jnp.float32
        ).astype(jnp.bfloat16)
        mixed_heads = split_heads(grad_mixed)
        grad_values = jnp.einsum(
            "ihst,sihe->tihe",
            probs.astype(jnp.bfloat16),
            mixed_heads,
            preferred_element_type=jnp.float32,
        ).astype(jnp.bfloat16)
        grad_prob = jnp.einsum(
            "sihe,tihe->ihst", mixed_heads, split_heads(values), preferred_element_type=jnp.float32
        )
        grad_score = (
            probs * (grad_prob - jnp.sum(grad_prob * probs, axis=-1, keepdims=True))
        ).astype(jnp.bfloat16)
        grad_query = (
            jnp.einsum(
                "ihst,tihe->sihe", grad_score, split_heads(keys), preferred_element_type=jnp.float32
            )
            * score_scale
        ).astype(jnp.bfloat16)
        grad_keys = (
            jnp.einsum(
                "ihst,sihe->tihe",
                grad_score,
                split_heads(query),
                preferred_element_type=jnp.float32,
            )
            * score_scale
        ).astype(jnp.bfloat16)
        flat_shape = query.shape
        grad_joined = jnp.stack(
            [
                grad_query.reshape(flat_shape),
                grad_keys.reshape(flat_shape),
                grad_values.reshape(flat_shape),
            ],
            axis=2,
        )
        query_b_grad = row_total(grad_query).reshape(-1)
        value_b_grad = row_total(grad_values).reshape(-1)
        qkv_w_grad = jnp.einsum(
            "sid,sicf->dcf", normed, grad_joined, preferred_element_type=jnp.float32
        )

        def qkv_back(start, count):
            return jnp.einsum(
                "sicf,dcf->sid", grad_joined, qkv_full, preferred_element_type=jnp.float32
            )

        first_value, first_pull = jax.vjp(layer_norm, hidden, gain_one, shift_one)
        hidden_part, gain_one_grad, shift_one_grad = first_pull(collect_grads(qkv_back))
        grad_in = grad_middle + hidden_part
        weight_grads = (qkv_w_grad, out_w_grad, up_w_grad, down_w_grad)
        vector_grads = (
            gain_one_grad,
            shift_one_grad,
            query_b_grad,
            value_b_grad,
            out_b_grad,
            gain_two_grad,
            shift_two_grad,
            up_b_grad,
            down_b_grad,
        )
        return (grad_in, weight_grads, vector_grads)

    def to_rows(array):
        return jnp.transpose(array.astype(jnp.float32), (2, 0, 1, 3)).reshape(
            local_rows, image_count, model_width
        )

    def from_rows(array):
        return jnp.transpose(
            array.reshape(local_rows, micro_count, slot_count, model_width), (1, 2, 0, 3)
        )

    live_flags = dealt.astype(jnp.float32).reshape(image_count)
    state = to_rows(tokens)
    gathered = []
    layer = 0
    weights = (
        lax.all_gather(qkv_weight[layer], "fsdp", axis=0, tiled=True),
        lax.all_gather(out_weight[layer], "fsdp", axis=0, tiled=True),
        lax.all_gather(up_weight[layer], "fsdp", axis=0, tiled=True),
        lax.all_gather(down_weight[layer], "fsdp", axis=0, tiled=True),
    )
    gathered.append(weights)
    vecs = vectors(layer)
    layer_inputs = [state]
    saved = inner_forward(state, weights, vecs)
    down_full = weights[3]
    activated = saved[9]

    def down_term(start, count):
        return jnp.einsum("sif,ef->sie", activated, down_full, preferred_element_type=jnp.float32)

    state = saved[6] + (collect_rows(down_term) + vecs[8])
    block_out = from_rows(state * live_flags[None, :, None]).astype(jnp.bfloat16)
    grad_state = to_rows(cotangent) * live_flags[None, :, None]
    weight_shards = [None] * layer_count
    vector_parts = [None] * layer_count
    for layer in reversed(range(layer_count)):
        weights = (
            lax.all_gather(qkv_weight[layer], "fsdp", axis=0, tiled=True),
            lax.all_gather(out_weight[layer], "fsdp", axis=0, tiled=True),
            lax.all_gather(up_weight[layer], "fsdp", axis=0, tiled=True),
            lax.all_gather(down_weight[layer], "fsdp", axis=0, tiled=True),
        )
        vecs = vectors(layer)
        grad_state, weight_totals, vector_totals = backward_layer(
            layer_inputs[layer], grad_state, weights, vecs
        )
        weight_shards[layer] = (
            lax.psum_scatter(
                weight_totals[0].astype(jnp.bfloat16), "fsdp", scatter_dimension=0, tiled=True
            ).astype(jnp.float32),
            lax.psum_scatter(
                weight_totals[1].astype(jnp.bfloat16), "fsdp", scatter_dimension=0, tiled=True
            ).astype(jnp.float32),
            lax.psum_scatter(
                weight_totals[2].astype(jnp.bfloat16), "fsdp", scatter_dimension=0, tiled=True
            ).astype(jnp.float32),
            lax.psum_scatter(
                weight_totals[3].astype(jnp.bfloat16), "fsdp", scatter_dimension=0, tiled=True
            ).astype(jnp.float32),
        )
        width_zero = jnp.zeros((model_width,), jnp.float32)
        unit_zero = jnp.zeros((unit_total,), jnp.float32)
        query_full = lax.dynamic_update_slice_in_dim(
            width_zero, vector_totals[2], tensor_index * head_cols, 0
        )
        value_full = lax.dynamic_update_slice_in_dim(
            width_zero, vector_totals[3], tensor_index * head_cols, 0
        )
        up_full_grad = lax.dynamic_update_slice_in_dim(
            unit_zero, vector_totals[7], tensor_index * unit_cols, 0
        )
        vector_parts[layer] = (
            vector_totals[0],
            vector_totals[1],
            query_full,
            value_full,
            vector_totals[4],
            vector_totals[5],
            vector_totals[6],
            up_full_grad,
            vector_totals[8],
        )
    input_grad = from_rows(grad_state).astype(jnp.bfloat16)
    stacked = [jnp.stack([vector_parts[0][index]]) for index in range(9)]
    summed = lax.psum(
        (
            stacked[0],
            stacked[1],
            stacked[2],
            stacked[3],
            stacked[4],
            stacked[5],
            stacked[6],
            stacked[7],
            stacked[8],
        ),
        ("fsdp", "tensor"),
    )
    qkv_grad = jnp.stack([weight_shards[0][0]])
    out_grad = jnp.stack([weight_shards[0][1]])
    up_grad = jnp.stack([weight_shards[0][2]])
    down_grad = jnp.stack([weight_shards[0][3]])
    return (
        block_out,
        input_grad,
        qkv_grad,
        out_grad,
        up_grad,
        down_grad,
        summed[0],
        summed[1],
        summed[2],
        summed[3],
        summed[4],
        summed[5],
        summed[6],
        summed[7],
        summed[8],
    )


def solution(mesh):
    placed = (
        P(None, "fsdp", "tensor", None),
        P(None, "fsdp"),
        P(None, "fsdp", "tensor", None),
        P(None, "fsdp", None, "tensor"),
        P(None, "fsdp", "tensor"),
        P(None, "fsdp", "tensor"),
        P(None, "fsdp", "tensor"),
        P(),
        P(),
        P(),
        P(),
        P(),
        P(),
        P(),
        P(),
        P(),
    )
    return jax.shard_map(
        local,
        mesh=mesh,
        in_specs=placed,
        out_specs=(
            P(None, "fsdp", "tensor", None),
            P(None, "fsdp", "tensor", None),
            P(None, "fsdp", None, "tensor"),
            P(None, "fsdp", "tensor"),
            P(None, "fsdp", "tensor"),
            P(None, "fsdp", "tensor"),
            P(),
            P(),
            P(),
            P(),
            P(),
            P(),
            P(),
            P(),
            P(),
        ),
        check_vma=False,
    )
```

profile of v0, /device:TPU:1, one launch (start us, length us, event | category | flops | bytes accessed | tf_op | source)
XLA Modules:
  0.0 1273.6 jit_solution(8190465983261844580)
XLA Ops:
  9.5 1.9 fusion.36
  13.8 86.5 %all-gather.1 = bf16[1,1024,256]{2,1,0:T(8,128)(2,1)S(1)} all-gather(bf16[1,32,256]{2,1,0:T(8,128)(2,1)} %param.20), channel_id=3, replica_groups=mesh['fsdp'=32,'tensor'=4] {'fsdp'}, dimensions={1}, use_global_device_ids=true | all-gather | bytes 540672 | tf_op jit(solution)/shard_map/all_gather | solution.py:250
  100.3 6.4 all-gather.20.cloned.1.call-done
  106.7 2.8 fusion.17
  116.2 29.6 %reduce-scatter.9.cloned.1.call-done = f32[64,2,1024]{2,0,1:T(8,128)} async-done(((f32[256,2,1024]{2,0,1:T(8,128)}), f32[64,2,1024]{2,0,1:T(8,128)}) %reduce-scatter.9.cloned.1.call-update) | async-done | bytes 524304 | tf_op jit(solution)/shard_map/reduce_scatter | solution.py:61
  150.0 69.4 %all-gather.22.cloned.1.call-done = bf16[1,1024,1024]{2,1,0:T(8,128)(2,1)} async-done(((bf16[1,32,1024]{2,1,0:T(8,128)(2,1)}), bf16[1,1024,1024]{2,1,0:T(8,128)(2,1)}) %all-gather.22.cloned.1.call-update) | async-done | bytes 2097168 | tf_op jit(solution)/shard_map/all_gather | solution.py:251
  219.4 21.5 %all-gather.14.cloned.1.call-done = bf16[256,2,1024]{2,0,1:T(8,128)(2,1)} async-done(((bf16[64,2,1024]{2,0,1:T(8,128)(2,1)}), bf16[256,2,1024]{2,0,1:T(8,128)(2,1)}) %all-gather.14.cloned.1.call-update) | async-done | bytes 1048592 | tf_op jit(solution)/shard_map/all_gather | solution.py:55
  240.9 3.8 fusion.49
  246.1 5.9 multiply_convert_fusion.1
  252.0 12.8 %all-gather.16.cloned.1.call-done = bf16[256,2,1024]{2,0,1:T(8,128)(2,1)} async-done(((bf16[64,2,1024]{2,0,1:T(8,128)(2,1)}), bf16[256,2,1024]{2,0,1:T(8,128)(2,1)}) %all-gather.16.cloned.1.call-update) | async-done | bytes 1048592 | tf_op jit(solution)/shard_map/all_gather | solution.py:58
  264.8 73.5 %all-gather.24.cloned.1.call-done = bf16[1,1024,1024]{2,1,0:T(8,128)(2,1)} async-done(((bf16[1,32,1024]{2,1,0:T(8,128)(2,1)}), bf16[1,1024,1024]{2,1,0:T(8,128)(2,1)}) %all-gather.24.cloned.1.call-update) | async-done | bytes 2097168 | tf_op jit(solution)/shard_map/all_gather | solution.py:252
  338.3 5.2 convert_reduce_fusion
  344.6 2.6 fusion.6
  347.4 4.2 fusion.4
  351.7 22.3 %reduce-scatter.13.cloned.1.call-done = f32[64,2,1024]{2,0,1:T(8,128)} async-done(((f32[256,2,1024]{2,0,1:T(8,128)}), f32[64,2,1024]{2,0,1:T(8,128)}) %reduce-scatter.13.cloned.1.call-update) | async-done | bytes 524304 | tf_op jit(solution)/shard_map/reduce_scatter | solution.py:69
  375.3 30.3 %reduce-scatter.11.cloned.1.call-done = f32[64,2,1024]{2,0,1:T(8,128)} async-done(((f32[256,2,1024]{2,0,1:T(8,128)}), f32[64,2,1024]{2,0,1:T(8,128)}) %reduce-scatter.11.cloned.1.call-update) | async-done | bytes 524304 | tf_op jit(solution)/shard_map/reduce_scatter | solution.py:61
  405.6 2.2 fusion.67
  408.7 4.1 bitcast_convert_fusion.1
  412.9 3.8 bitcast_convert_fusion
  416.9 13.8 %all-gather.18.cloned.1.call-done = bf16[256,2,1024]{2,0,1:T(8,128)(2,1)} async-done(((bf16[64,2,1024]{2,0,1:T(8,128)(2,1)}), bf16[256,2,1024]{2,0,1:T(8,128)(2,1)}) %all-gather.18.cloned.1.call-update) | async-done | bytes 1048592 | tf_op jit(solution)/shard_map/all_gather | solution.py:58
  432.4 2.5 fusion.21
  434.9 2.4 multiply_reduce_fusion
  439.3 2.1 convert_reduce_fusion.3
  441.6 3.5 bitcast_convert_fusion.2
  445.2 2.4 convolution_bitcast_fusion
  447.7 149.5 %reduce-scatter.21.cloned.1.call-done = bf16[32,1024]{1,0:T(8,128)(2,1)} async-done(((bf16[1024,1024]{1,0:T(8,128)(2,1)}), bf16[32,1024]{1,0:T(8,128)(2,1)}) %reduce-scatter.21.cloned.1.call-update) | async-done | bytes 65552 | tf_op jit(solution)/shard_map/reduce_scatter | solution.py:287
  598.6 183.4 %reduce-scatter.23.cloned.1.call-done = bf16[32,1024]{1,0:T(8,128)(2,1)} async-done(((bf16[1024,1024]{1,0:T(8,128)(2,1)}), bf16[32,1024]{1,0:T(8,128)(2,1)}) %reduce-scatter.23.cloned.1.call-update) | async-done | bytes 65552 | tf_op jit(solution)/shard_map/reduce_scatter | solution.py:290
  783.7 177.1 %reduce-scatter.19.cloned.1.call-done = bf16[32,256]{1,0:T(8,128)(2,1)} async-done(((bf16[1024,256]{1,0:T(8,128)(2,1)}), bf16[32,256]{1,0:T(8,128)(2,1)}) %reduce-scatter.19.cloned.1.call-update) | async-done | bytes 16400 | tf_op jit(solution)/shard_map/reduce_scatter | solution.py:284
  962.2 183.6 %reduce-scatter.17.cloned.1.call-done = bf16[32,3,256]{2,0,1:T(8,128)(2,1)} async-done(((bf16[1024,3,256]{2,0,1:T(8,128)(2,1)}), bf16[32,3,256]{2,0,1:T(8,128)(2,1)}) %reduce-scatter.17.cloned.1.call-update) | async-done | bytes 49168 | tf_op jit(solution)/shard_map/reduce_scatter | solution.py:281
  1147.2 48.5 %reduce-scatter.15.cloned.1.call-done = f32[64,2,1024]{2,0,1:T(8,128)} async-done(((f32[256,2,1024]{2,0,1:T(8,128)}), f32[64,2,1024]{2,0,1:T(8,128)}) %reduce-scatter.15.cloned.1.call-update) | async-done | bytes 524304 | tf_op jit(solution)/shard_map/reduce_scatter | solution.py:69
  1198.4 66.6 %all-reduce = (f32[1,1024]{1,0:T(1,128)}, f32[1,1024]{1,0:T(1,128)}, f32[1,1024]{1,0:T(1,128)}, f32[1,1024]{1,0:T(1,128)}, f32[1,1024]{1,0:T(1,128)}, /*index=5*...) all-reduce(f32[1,1024]{1,0:T(1,128)S(1)} %bitcast.237, ...), channel_id=1, replica_groups=mesh['fsdp'=32,'tensor'=4] {'fsdp','tensor'}, use_global_device_ids=true, to_apply=%region_20.0 | all-reduce | flops 12288 | bytes 98304 | tf_op jit(solution)/shard_map/psum | solution.py:318
  1265.1 2.0 fusion.52
  (119 shorter events, 33.0 us)
Async XLA Ops:
  7.2 142.8 %copy-start = (f32[1,4096]{1,0:T(1,128)S(1)}, f32[1,4096]{1,0:T(1,128)}, u32[]{:S(2)}) copy-start(f32[1,4096]{1,0:T(1,128)} %param.30) | copy-start | bytes 49156
  7.2 93.1 %all-gather.12.cloned.1.call-start = ((), (), s32[]{:S(2)}) async-start(), calls=%async_computation.8 | async-start | bytes 1310720 | tf_op jit(solution)/shard_map/all_gather | solution.py:55
  11.4 95.3 %all-gather.20.cloned.1.call-start = ((), (), s32[]{:S(2)}) async-start(), calls=%async_computation.20 | async-start | bytes 1622016 | tf_op jit(solution)/shard_map/all_gather | solution.py:249
  12.2 133.7 %reduce-scatter.9.cloned.1.call-start = ((), (), s32[]{:S(2)}) async-start(), calls=%async_computation.9 | async-start | bytes 2621440 | tf_op jit(solution)/shard_map/reduce_scatter | solution.py:61
  110.3 2.7 copy-start.6
  111.3 1.8 copy-start.3
  113.8 32.1 %copy-start.1 = (bf16[2,1,64,1024]{3,2,1,0:T(8,128)(2,1)S(1)}, bf16[2,1,64,1024]{3,2,1,0:T(8,128)(2,1)}, u32[]{:S(2)}) copy-start(bf16[2,1,64,1024]{3,2,1,0:T(8,128)(2,1)} %param.16) | copy-start | bytes 786436
  113.8 32.1 %copy-start.13 = (f32[1,1024]{1,0:T(1,128)S(1)}, f32[1,1024]{1,0:T(1,128)}, u32[]{:S(2)}) copy-start(f32[1,1024]{1,0:T(1,128)} %param.27) | copy-start | bytes 12292
  115.6 31.7 %copy-start.12 = (f32[1,1024]{1,0:T(1,128)S(1)}, f32[1,1024]{1,0:T(1,128)}, u32[]{:S(2)}) copy-start(f32[1,1024]{1,0:T(1,128)} %param.28) | copy-start | bytes 12292
  115.6 31.7 %copy-start.14 = (f32[1,1024]{1,0:T(1,128)S(1)}, f32[1,1024]{1,0:T(1,128)}, u32[]{:S(2)}) copy-start(f32[1,1024]{1,0:T(1,128)} %param.29) | copy-start | bytes 12292
  115.6 32.7 %copy-start.18 = (s32[2,1]{0,1:T(1,128)S(1)}, s32[2,1]{0,1:T(1,128)}, u32[]{:S(2)}) copy-start(s32[2,1]{0,1:T(1,128)} %param.17) | copy-start | bytes 28
  115.6 32.7 %copy-start.2 = (bf16[2,1,64,1024]{3,2,1,0:T(8,128)(2,1)S(1)}, bf16[2,1,64,1024]{3,2,1,0:T(8,128)(2,1)}, u32[]{:S(2)}) copy-start(bf16[2,1,64,1024]{3,2,1,0:T(8,128)(2,1)} %param.18) | copy-start | bytes 786436
  115.6 103.8 %all-gather.22.cloned.1.call-start = ((), (), s32[]{:S(2)}) async-start(), calls=%async_computation.21 | async-start | bytes 2162688 | tf_op jit(solution)/shard_map/all_gather | solution.py:251
  116.2 124.7 %all-gather.14.cloned.1.call-start = ((), (), s32[]{:S(2)}) async-start(), calls=%async_computation.10 | async-start | bytes 1310720 | tf_op jit(solution)/shard_map/all_gather | solution.py:55
  148.2 116.6 %all-gather.16.cloned.1.call-start = ((), (), s32[]{:S(2)}) async-start(), calls=%async_computation.12 | async-start | bytes 1310720 | tf_op jit(solution)/shard_map/all_gather | solution.py:58
  149.1 189.1 %all-gather.24.cloned.1.call-start = ((), (), s32[]{:S(2)}) async-start(), calls=%async_computation.22 | async-start | bytes 2162688 | tf_op jit(solution)/shard_map/all_gather | solution.py:252
  149.9 224.1 %reduce-scatter.13.cloned.1.call-start = ((), (), s32[]{:S(2)}) async-start(), calls=%async_computation.13 | async-start | bytes 2621440 | tf_op jit(solution)/shard_map/reduce_scatter | solution.py:69
  244.7 1.4 copy-start.5
  338.3 6.3 copy-start.16
  347.2 58.4 %reduce-scatter.11.cloned.1.call-start = ((), (), s32[]{:S(2)}) async-start(), calls=%async_computation.11 | async-start | bytes 2621440 | tf_op jit(solution)/shard_map/reduce_scatter | solution.py:61
  351.6 54.0 %copy-start.15 = (f32[1,1024]{1,0:T(1,128)S(1)}, f32[1,1024]{1,0:T(1,128)}, u32[]{:S(2)}) copy-start(f32[1,1024]{1,0:T(1,128)} %param.31) | copy-start | bytes 12292
  351.6 79.0 %all-gather.18.cloned.1.call-start = ((), (), s32[]{:S(2)}) async-start(), calls=%async_computation.14 | async-start | bytes 1310720 | tf_op jit(solution)/shard_map/all_gather | solution.py:58
  408.7 188.4 %reduce-scatter.21.cloned.1.call-start = ((), (), s32[]{:S(2)}) async-start(), calls=%async_computation.18 | async-start | bytes 2162688 | tf_op jit(solution)/shard_map/reduce_scatter | solution.py:287
  412.9 369.1 %reduce-scatter.23.cloned.1.call-start = ((), (), s32[]{:S(2)}) async-start(), calls=%async_computation.19 | async-start | bytes 2162688 | tf_op jit(solution)/shard_map/reduce_scatter | solution.py:290
  416.8 15.6 %copy-start.9 = (bf16[2,4,64,256]{3,2,1,0:T(8,128)(2,1)S(1)}, bf16[2,4,64,256]{3,2,1,0:T(8,128)(2,1)}, u32[]{:S(2)}) copy-start(bf16[2,4,64,256]{3,2,1,0:T(8,128)(2,1)} %copy-done.8) | copy-start | bytes 786436
  416.8 18.1 %copy-start.10 = (f32[256,2,1,256]{0,3,2,1:T(8,128)S(1)}, f32[256,2,1,256]{0,3,2,1:T(8,128)}, u32[]{:S(2)}) copy-start(f32[256,2,1,256]{0,3,2,1:T(8,128)} %get-tuple-element.74) | copy-start | bytes 1572868
  416.8 544.0 %reduce-scatter.19.cloned.1.call-start = ((), (), s32[]{:S(2)}) async-start(), calls=%async_computation.17 | async-start | bytes 540672 | tf_op jit(solution)/shard_map/reduce_scatter | solution.py:284
  434.9 2.4 copy-start.4
  437.7 708.1 %reduce-scatter.17.cloned.1.call-start = ((), (), s32[]{:S(2)}) async-start(), calls=%async_computation.16 | async-start | bytes 1622016 | tf_op jit(solution)/shard_map/reduce_scatter | solution.py:281
  441.6 3.6 copy-start.17
  445.2 750.6 %reduce-scatter.15.cloned.1.call-start = ((), (), s32[]{:S(2)}) async-start(), calls=%async_computation.15 | async-start | bytes 2621440 | tf_op jit(solution)/shard_map/reduce_scatter | solution.py:69
  447.6 748.2 %copy-start.11 = (f32[1,1024]{1,0:T(1,128)S(1)}, f32[1,1024]{1,0:T(1,128)}, u32[]{:S(2)}) copy-start(f32[1,1024]{1,0:T(1,128)} %param.23) | copy-start | bytes 12292
  (3 other events, 2.8 us)
Sparse Core Ops, SparseCore 0:
  11.6 24.4 all-gather.11
  39.1 67.5 all-gather.19
  115.7 30.0 reduce-scatter.8
  149.2 70.1 all-gather.21
  221.6 19.2 all-gather.13
  243.1 21.6 all-gather.15
  268.2 70.0 all-gather.23
  347.3 26.6 reduce-scatter.12
  376.4 29.1 reduce-scatter.10
  408.8 21.8 all-gather.17
  433.1 163.9 reduce-scatter.20
  599.3 182.6 reduce-scatter.22
  784.5 176.3 reduce-scatter.18
  963.1 182.6 reduce-scatter.16
  1148.2 47.5 reduce-scatter.14
where the time goes:
time: 1270 us
  waiting for transfers between devices  1020 us (80%)
  blocking collectives  153 us (12%)
  matrix products  46.5 us (4%)
  other arithmetic  28.4 us (2%)
  between operations  14.2 us (1%)
    reduce_scatter x1, waiting for transfers between devices, local(): lax.psum_scatter(weight_totals[0].astype(jnp.bfloat16), 'fsdp', scatter_d...  184 us
    reduce_scatter x1, waiting for transfers between devices, local(): lax.psum_scatter(weight_totals[3].astype(jnp.bfloat16), 'fsdp', scatter_d...  183 us
    reduce_scatter x1, waiting for transfers between devices, local(): lax.psum_scatter(weight_totals[1].astype(jnp.bfloat16), 'fsdp', scatter_d...  177 us
    reduce_scatter x1, waiting for transfers between devices, local(): lax.psum_scatter(weight_totals[2].astype(jnp.bfloat16), 'fsdp', scatter_d...  149 us
    all_gather x1, blocking collectives, local(): lax.all_gather(out_weight[layer], 'fsdp', axis=0, tiled=True)  86.5 us
    all_gather x1, waiting for transfers between devices, local(): lax.all_gather(down_weight[layer], 'fsdp', axis=0, tiled=True)  73.5 us
    reduce_scatter x2, waiting for transfers between devices, collect_grads(): lax.psum_scatter(term_fn(jnp.int32(0), local_rows * lax.axis_size('tensor...  70.8 us
    all_gather x1, waiting for transfers between devices, local(): lax.all_gather(up_weight[layer], 'fsdp', axis=0, tiled=True)  69.4 us
  transfers between devices with their start and end apart: 15, of which 14 were waited for; matrix products, arithmetic and copies ran while one was open for 4% of the time, Pallas kernels for 0%

commit v1 on v0

--- a/solution.py
+++ b/solution.py
@@ -316,18 +316,21 @@
     input_grad = from_rows(grad_state).astype(jnp.bfloat16)
     stacked = [jnp.stack([vector_parts[0][index]]) for index in range(9)]
     summed = lax.psum(
-        (
-            stacked[0],
-            stacked[1],
-            stacked[2],
-            stacked[3],
-            stacked[4],
-            stacked[5],
-            stacked[6],
-            stacked[7],
-            stacked[8],
+        lax.psum(
+            (
+                stacked[0],
+                stacked[1],
+                stacked[2],
+                stacked[3],
+                stacked[4],
+                stacked[5],
+                stacked[6],
+                stacked[7],
+                stacked[8],
+            ),
+            "tensor",
         ),
-        ("fsdp", "tensor"),
+        "fsdp",
     )
     qkv_grad = jnp.stack([weight_shards[0][0]])
     out_grad = jnp.stack([weight_shards[0][1]])

time: 1270 us -> 1400 us (1.10)
  the two profiles are of different devices: /device:TPU:1 before, /device:TPU:0 now
where the time goes in v1:
time: 1400 us
  waiting for transfers between devices  1010 us (72%)
  blocking collectives  294 us (21%)
  matrix products  46.5 us (3%)
  other arithmetic  27.4 us (2%)
  between operations  14.2 us (1%)
    psum x1, blocking collectives, local(): lax.psum(lax.psum((stacked[0], stacked[1], stacked[2], stacked[3], stacke...  184 us
    reduce_scatter x1, waiting for transfers between devices, local(): lax.psum_scatter(weight_totals[3].astype(jnp.bfloat16), 'fsdp', scatter_d...  183 us
    reduce_scatter x1, waiting for transfers between devices, local(): lax.psum_scatter(weight_totals[0].astype(jnp.bfloat16), 'fsdp', scatter_d...  182 us
    reduce_scatter x1, waiting for transfers between devices, local(): lax.psum_scatter(weight_totals[1].astype(jnp.bfloat16), 'fsdp', scatter_d...  180 us
    reduce_scatter x1, waiting for transfers between devices, local(): lax.psum_scatter(weight_totals[2].astype(jnp.bfloat16), 'fsdp', scatter_d...  174 us
    all_gather x1, blocking collectives, local(): lax.all_gather(out_weight[layer], 'fsdp', axis=0, tiled=True)  99.9 us
    all_gather x1, waiting for transfers between devices, local(): lax.all_gather(down_weight[layer], 'fsdp', axis=0, tiled=True)  75.3 us
    all_gather x1, waiting for transfers between devices, local(): lax.all_gather(up_weight[layer], 'fsdp', axis=0, tiled=True)  71.1 us
  transfers between devices with their start and end apart: 15, of which 13 were waited for; matrix products, arithmetic and copies ran while one was open for 4% of the time, Pallas kernels for 0%

profile of v1, /device:TPU:0, one launch (start us, length us, event | category | flops | bytes accessed | tf_op | source)
XLA Modules:
  0.0 1399.4 jit_solution(297948855442923770)
XLA Ops:
  9.5 1.9 fusion.36
  13.8 99.9 %all-gather.1 = bf16[1,1024,256]{2,1,0:T(8,128)(2,1)S(1)} all-gather(bf16[1,32,256]{2,1,0:T(8,128)(2,1)} %param.20), channel_id=3, replica_groups=mesh['fsdp'=32,'tensor'=4] {'fsdp'}, dimensions={1}, use_global_device_ids=true | all-gather | bytes 540672 | tf_op jit(solution)/shard_map/all_gather | solution.py:250
  113.7 2.8 fusion.17
  120.8 1.8 fusion.42
  123.3 21.6 %reduce-scatter.9.cloned.1.call-done = f32[64,2,1024]{2,0,1:T(8,128)} async-done(((f32[256,2,1024]{2,0,1:T(8,128)}), f32[64,2,1024]{2,0,1:T(8,128)}) %reduce-scatter.9.cloned.1.call-update) | async-done | bytes 524304 | tf_op jit(solution)/shard_map/reduce_scatter | solution.py:61
  148.9 71.1 %all-gather.22.cloned.1.call-done = bf16[1,1024,1024]{2,1,0:T(8,128)(2,1)} async-done(((bf16[1,32,1024]{2,1,0:T(8,128)(2,1)}), bf16[1,1024,1024]{2,1,0:T(8,128)(2,1)}) %all-gather.22.cloned.1.call-update) | async-done | bytes 2097168 | tf_op jit(solution)/shard_map/all_gather | solution.py:251
  220.0 19.7 %all-gather.14.cloned.1.call-done = bf16[256,2,1024]{2,0,1:T(8,128)(2,1)} async-done(((bf16[64,2,1024]{2,0,1:T(8,128)(2,1)}), bf16[256,2,1024]{2,0,1:T(8,128)(2,1)}) %all-gather.14.cloned.1.call-update) | async-done | bytes 1048592 | tf_op jit(solution)/shard_map/all_gather | solution.py:55
  239.7 3.8 fusion.49
  244.9 5.9 multiply_convert_fusion.1
  250.8 12.8 all-gather.16.cloned.1.call-done
  263.6 75.3 %all-gather.24.cloned.1.call-done = bf16[1,1024,1024]{2,1,0:T(8,128)(2,1)} async-done(((bf16[1,32,1024]{2,1,0:T(8,128)(2,1)}), bf16[1,1024,1024]{2,1,0:T(8,128)(2,1)}) %all-gather.24.cloned.1.call-update) | async-done | bytes 2097168 | tf_op jit(solution)/shard_map/all_gather | solution.py:252
  338.9 5.2 convert_reduce_fusion
  345.2 2.6 fusion.6
  348.0 4.2 fusion.4
  352.3 20.6 %reduce-scatter.13.cloned.1.call-done = f32[64,2,1024]{2,0,1:T(8,128)} async-done(((f32[256,2,1024]{2,0,1:T(8,128)}), f32[64,2,1024]{2,0,1:T(8,128)}) %reduce-scatter.13.cloned.1.call-update) | async-done | bytes 524304 | tf_op jit(solution)/shard_map/reduce_scatter | solution.py:69
  374.2 30.3 %reduce-scatter.11.cloned.1.call-done = f32[64,2,1024]{2,0,1:T(8,128)} async-done(((f32[256,2,1024]{2,0,1:T(8,128)}), f32[64,2,1024]{2,0,1:T(8,128)}) %reduce-scatter.11.cloned.1.call-update) | async-done | bytes 524304 | tf_op jit(solution)/shard_map/reduce_scatter | solution.py:61
  404.6 2.2 fusion.67
  407.7 4.1 bitcast_convert_fusion.1
  411.9 3.8 bitcast_convert_fusion
  415.9 13.6 all-gather.18.cloned.1.call-done
  431.2 2.5 fusion.21
  433.7 2.4 multiply_reduce_fusion
  438.1 2.1 convert_reduce_fusion.3
  440.4 3.5 bitcast_convert_fusion.2
  444.0 2.4 convolution_bitcast_fusion
  446.5 173.9 %reduce-scatter.21.cloned.1.call-done = bf16[32,1024]{1,0:T(8,128)(2,1)} async-done(((bf16[1024,1024]{1,0:T(8,128)(2,1)}), bf16[32,1024]{1,0:T(8,128)(2,1)}) %reduce-scatter.21.cloned.1.call-update) | async-done | bytes 65552 | tf_op jit(solution)/shard_map/reduce_scatter | solution.py:287
  621.8 182.9 %reduce-scatter.23.cloned.1.call-done = bf16[32,1024]{1,0:T(8,128)(2,1)} async-done(((bf16[1024,1024]{1,0:T(8,128)(2,1)}), bf16[32,1024]{1,0:T(8,128)(2,1)}) %reduce-scatter.23.cloned.1.call-update) | async-done | bytes 65552 | tf_op jit(solution)/shard_map/reduce_scatter | solution.py:290
  806.4 179.8 %reduce-scatter.19.cloned.1.call-done = bf16[32,256]{1,0:T(8,128)(2,1)} async-done(((bf16[1024,256]{1,0:T(8,128)(2,1)}), bf16[32,256]{1,0:T(8,128)(2,1)}) %reduce-scatter.19.cloned.1.call-update) | async-done | bytes 16400 | tf_op jit(solution)/shard_map/reduce_scatter | solution.py:284
  987.6 181.8 %reduce-scatter.17.cloned.1.call-done = bf16[32,3,256]{2,0,1:T(8,128)(2,1)} async-done(((bf16[1024,3,256]{2,0,1:T(8,128)(2,1)}), bf16[32,3,256]{2,0,1:T(8,128)(2,1)}) %reduce-scatter.17.cloned.1.call-update) | async-done | bytes 49168 | tf_op jit(solution)/shard_map/reduce_scatter | solution.py:281
  1170.8 23.9 %reduce-scatter.15.cloned.1.call-done = f32[64,2,1024]{2,0,1:T(8,128)} async-done(((f32[256,2,1024]{2,0,1:T(8,128)}), f32[64,2,1024]{2,0,1:T(8,128)}) %reduce-scatter.15.cloned.1.call-update) | async-done | bytes 524304 | tf_op jit(solution)/shard_map/reduce_scatter | solution.py:69
  1197.5 10.6 all-reduce.1
  1208.1 183.8 %all-reduce = (f32[1,1024]{1,0:T(1,128)}, f32[1,1024]{1,0:T(1,128)}, f32[1,1024]{1,0:T(1,128)}, f32[1,1024]{1,0:T(1,128)}, f32[1,1024]{1,0:T(1,128)}, /*index=5*...) all-reduce(f32[1,1024]{1,0:T(1,128)S(1)} %get-tuple-element.63, ...), channel_id=1, replica_groups=mesh['fsdp'=32,'tensor'=4] {'fsdp'}, use_global_device_ids=true, to_apply=%region_21.0 | all-reduce | flops 12288 | bytes 98304 | tf_op jit(solution)/shard_map/psum | solution.py:318
  (122 shorter events, 32.3 us)
Async XLA Ops:
  7.2 141.7 %copy-start = (f32[1,4096]{1,0:T(1,128)S(1)}, f32[1,4096]{1,0:T(1,128)}, u32[]{:S(2)}) copy-start(f32[1,4096]{1,0:T(1,128)} %param.30) | copy-start | bytes 49156
  7.2 106.5 %all-gather.12.cloned.1.call-start = ((), (), s32[]{:S(2)}) async-start(), calls=%async_computation.8 | async-start | bytes 1310720 | tf_op jit(solution)/shard_map/all_gather | solution.py:55
  11.4 102.3 %all-gather.20.cloned.1.call-start = ((), (), s32[]{:S(2)}) async-start(), calls=%async_computation.20 | async-start | bytes 1622016 | tf_op jit(solution)/shard_map/all_gather | solution.py:249
  12.2 132.7 %reduce-scatter.9.cloned.1.call-start = ((), (), s32[]{:S(2)}) async-start(), calls=%async_computation.9 | async-start | bytes 2621440 | tf_op jit(solution)/shard_map/reduce_scatter | solution.py:61
  117.4 2.7 copy-start.7
  118.3 1.8 copy-start.4
  120.8 24.1 %copy-start.1 = (bf16[2,1,64,1024]{3,2,1,0:T(8,128)(2,1)S(1)}, bf16[2,1,64,1024]{3,2,1,0:T(8,128)(2,1)}, u32[]{:S(2)}) copy-start(bf16[2,1,64,1024]{3,2,1,0:T(8,128)(2,1)} %param.16) | copy-start | bytes 786436
  120.8 24.1 %copy-start.14 = (f32[1,1024]{1,0:T(1,128)S(1)}, f32[1,1024]{1,0:T(1,128)}, u32[]{:S(2)}) copy-start(f32[1,1024]{1,0:T(1,128)} %param.27) | copy-start | bytes 12292
  122.6 23.7 %copy-start.13 = (f32[1,1024]{1,0:T(1,128)S(1)}, f32[1,1024]{1,0:T(1,128)}, u32[]{:S(2)}) copy-start(f32[1,1024]{1,0:T(1,128)} %param.28) | copy-start | bytes 12292
  122.6 23.7 %copy-start.15 = (f32[1,1024]{1,0:T(1,128)S(1)}, f32[1,1024]{1,0:T(1,128)}, u32[]{:S(2)}) copy-start(f32[1,1024]{1,0:T(1,128)} %param.29) | copy-start | bytes 12292
  122.6 24.6 %copy-start.19 = (s32[2,1]{0,1:T(1,128)S(1)}, s32[2,1]{0,1:T(1,128)}, u32[]{:S(2)}) copy-start(s32[2,1]{0,1:T(1,128)} %param.17) | copy-start | bytes 28
  122.6 24.6 %copy-start.3 = (bf16[2,1,64,1024]{3,2,1,0:T(8,128)(2,1)S(1)}, bf16[2,1,64,1024]{3,2,1,0:T(8,128)(2,1)}, u32[]{:S(2)}) copy-start(bf16[2,1,64,1024]{3,2,1,0:T(8,128)(2,1)} %param.18) | copy-start | bytes 786436
  122.7 97.4 %all-gather.22.cloned.1.call-start = ((), (), s32[]{:S(2)}) async-start(), calls=%async_computation.21 | async-start | bytes 2162688 | tf_op jit(solution)/shard_map/all_gather | solution.py:251
  123.2 116.5 %all-gather.14.cloned.1.call-start = ((), (), s32[]{:S(2)}) async-start(), calls=%async_computation.10 | async-start | bytes 1310720 | tf_op jit(solution)/shard_map/all_gather | solution.py:55
  147.2 116.4 %all-gather.16.cloned.1.call-start = ((), (), s32[]{:S(2)}) async-start(), calls=%async_computation.12 | async-start | bytes 1310720 | tf_op jit(solution)/shard_map/all_gather | solution.py:58
  148.1 190.8 %all-gather.24.cloned.1.call-start = ((), (), s32[]{:S(2)}) async-start(), calls=%async_computation.22 | async-start | bytes 2162688 | tf_op jit(solution)/shard_map/all_gather | solution.py:252
  148.9 224.1 %reduce-scatter.13.cloned.1.call-start = ((), (), s32[]{:S(2)}) async-start(), calls=%async_computation.13 | async-start | bytes 2621440 | tf_op jit(solution)/shard_map/reduce_scatter | solution.py:69
  338.9 6.3 copy-start.17
  347.8 56.8 %reduce-scatter.11.cloned.1.call-start = ((), (), s32[]{:S(2)}) async-start(), calls=%async_computation.11 | async-start | bytes 2621440 | tf_op jit(solution)/shard_map/reduce_scatter | solution.py:61
  352.2 52.3 %copy-start.16 = (f32[1,1024]{1,0:T(1,128)S(1)}, f32[1,1024]{1,0:T(1,128)}, u32[]{:S(2)}) copy-start(f32[1,1024]{1,0:T(1,128)} %param.31) | copy-start | bytes 12292
  352.3 77.2 %all-gather.18.cloned.1.call-start = ((), (), s32[]{:S(2)}) async-start(), calls=%async_computation.14 | async-start | bytes 1310720 | tf_op jit(solution)/shard_map/all_gather | solution.py:58
  407.7 212.7 %reduce-scatter.21.cloned.1.call-start = ((), (), s32[]{:S(2)}) async-start(), calls=%async_computation.18 | async-start | bytes 2162688 | tf_op jit(solution)/shard_map/reduce_scatter | solution.py:287
  411.9 392.8 %reduce-scatter.23.cloned.1.call-start = ((), (), s32[]{:S(2)}) async-start(), calls=%async_computation.19 | async-start | bytes 2162688 | tf_op jit(solution)/shard_map/reduce_scatter | solution.py:290
  415.8 15.4 %copy-start.10 = (bf16[2,4,64,256]{3,2,1,0:T(8,128)(2,1)S(1)}, bf16[2,4,64,256]{3,2,1,0:T(8,128)(2,1)}, u32[]{:S(2)}) copy-start(bf16[2,4,64,256]{3,2,1,0:T(8,128)(2,1)} %copy-done.9) | copy-start | bytes 786436
  415.8 17.9 %copy-start.11 = (f32[256,2,1,256]{0,3,2,1:T(8,128)S(1)}, f32[256,2,1,256]{0,3,2,1:T(8,128)}, u32[]{:S(2)}) copy-start(f32[256,2,1,256]{0,3,2,1:T(8,128)} %get-tuple-element.83) | copy-start | bytes 1572868
  415.8 570.4 %reduce-scatter.19.cloned.1.call-start = ((), (), s32[]{:S(2)}) async-start(), calls=%async_computation.17 | async-start | bytes 540672 | tf_op jit(solution)/shard_map/reduce_scatter | solution.py:284
  433.7 2.4 copy-start.5
  436.6 732.8 %reduce-scatter.17.cloned.1.call-start = ((), (), s32[]{:S(2)}) async-start(), calls=%async_computation.16 | async-start | bytes 1622016 | tf_op jit(solution)/shard_map/reduce_scatter | solution.py:281
  440.4 3.6 copy-start.18
  444.0 750.8 %reduce-scatter.15.cloned.1.call-start = ((), (), s32[]{:S(2)}) async-start(), calls=%async_computation.15 | async-start | bytes 2621440 | tf_op jit(solution)/shard_map/reduce_scatter | solution.py:69
  446.4 748.3 %copy-start.12 = (f32[1,1024]{1,0:T(1,128)S(1)}, f32[1,1024]{1,0:T(1,128)}, u32[]{:S(2)}) copy-start(f32[1,1024]{1,0:T(1,128)} %param.23) | copy-start | bytes 12292
  1194.7 197.1 %copy-start.2 = (f32[64,2,1024]{2,0,1:T(8,128)S(1)}, f32[64,2,1024]{2,0,1:T(8,128)}, u32[]{:S(2)}) copy-start(f32[64,2,1024]{2,0,1:T(8,128)} %reduce-scatter.15.cloned.1.call-done) | copy-start | bytes 1572868
  (4 other events, 4.2 us)
Sparse Core Ops, SparseCore 0:
  11.6 23.1 all-gather.11
  37.7 69.8 all-gather.19
  122.8 22.0 reduce-scatter.8
  148.1 71.8 all-gather.21
  222.2 17.4 all-gather.13
  241.9 21.6 all-gather.15
  267.0 71.8 all-gather.23
  347.9 24.9 reduce-scatter.12
  375.4 29.1 reduce-scatter.10
  407.8 21.6 all-gather.17
  432.0 188.3 reduce-scatter.20
  622.6 182.1 reduce-scatter.22
  807.2 179.0 reduce-scatter.18
  988.5 180.8 reduce-scatter.16
  1171.8 22.9 reduce-scatter.14
